TPU v7x, 512 devices: a whole 4x8x8 slice. The times are simulated.
512 devices in a mesh: aux: 64 (over z, y), bas: 8 (over x, core).
Axes of the slice: x: 4, y: 8, z: 8, core: 2. Of those that a mesh axis runs over, the one named last changes fastest.
Arguments:
- integrals: bfloat16 [64, 48, 16, 128, 128], P('aux', 'bas'), may hold values from -6 to 6
- coefficients: bfloat16 [6144, 1024], P(('aux', 'bas')), may hold values from -0.125 to 0.125
- metric: bfloat16 [64, 64], replicated, may hold values from -0.75 to 0.75
- pair_blocks: int32 [48, 16], P('bas'), may hold values from 0 to 47, as said below
- pair_live: int32 [48, 16], P('bas'), may hold values 0 or 1
Outputs:
- exchange_rows: float32 [512, 6144], P('aux', 'bas')
Inputs may be any that keep to these rules, and one draw needn't show every extreme that they name: `pair_blocks`: within one row the 16 block numbers are different.
All inputs are finite; a program needn't handle non-finite values. No bound on the sum of `pair_live` on one device may be relied on, other than what follows from the above.
Results may differ from a plain program's by a relative error of at most 0.0024.
Values may be sent and summed in bfloat16 or wider, within the bound.
A program may use at most 128 MiB of HBM per device.

v0:
```python
import math

import jax
import jax.numpy as jnp
from jax import lax
from jax.sharding import PartitionSpec as P

KROWS = 512


def spread(value, axis, root):
    mine = lax.axis_index(axis) == root
    return lax.psum(jnp.where(mine, value, jnp.zeros_like(value)), axis)


def on_device(integrals, coefficients, metric, pair_blocks, pair_live):
    tile_size = integrals.shape[-1]
    orbitals = coefficients.shape[1]
    aux_total = metric.shape[0]
    aux_local = integrals.shape[0]
    gathered = lax.all_gather(coefficients, ("aux", "bas"), axis=0, tiled=True)
    coeff_tiles = gathered.reshape(gathered.shape[0] // tile_size, tile_size, orbitals)

    def one_row(pieces):
        ints_row, lam_row, live_row = pieces
        picked = coeff_tiles[lam_row] * live_row.astype(jnp.bfloat16)[:, None, None]
        done = jnp.einsum("pzab,zbo->poa", ints_row, picked, preferred_element_type=jnp.float32)
        return done.astype(jnp.bfloat16)

    stacked = lax.map(one_row, (jnp.moveaxis(integrals, 1, 0), pair_blocks, pair_live))
    half_done = jnp.transpose(stacked, (1, 2, 0, 3)).reshape(aux_local, orbitals, -1)
    items = lax.all_to_all(half_done, "aux", split_axis=1, concat_axis=0, tiled=True)
    flat_items = items.reshape(aux_total, -1)
    mixed_items = jnp.dot(metric, flat_items, preferred_element_type=jnp.float32)
    regrouped = mixed_items.astype(jnp.bfloat16).reshape(items.shape)
    window = spread(regrouped[:, :, :KROWS], "bas", 0)
    contraction = regrouped.shape[0] * regrouped.shape[1]
    flat_all = regrouped.reshape(contraction, -1)
    flat_window = window.reshape(contraction, -1)
    factor = 1.0 / math.sqrt(aux_total * orbitals)
    return lax.psum_scatter(
        jnp.dot(flat_window.T, flat_all, preferred_element_type=jnp.float32) * factor,
        "aux",
        scatter_dimension=0,
        tiled=True,
    )


def solution(mesh):
    return jax.shard_map(
        on_device,
        mesh=mesh,
        in_specs=(
            P("aux", "bas", None, None, None),
            P(("aux", "bas"), None),
            P(),
            P("bas", None),
            P("bas", None),
        ),
        out_specs=P("aux", "bas"),
        check_vma=False,
    )
```

profile of v0, /device:TPU:1, one launch (start us, length us, event | category | flops | bytes accessed | tf_op | source)
XLA Modules:
  0.0 588.6 jit_solution(7769850167232382895)
XLA Ops:
  7.3 146.0 %all-gather.3.cloned.1.call-done = bf16[512,12,1024]{2,1,0:T(8,128)(2,1)} async-done(((bf16[1,12,1024]{2,1,0:T(8,128)(2,1)}), bf16[512,12,1024]{2,1,0:T(8,128)(2,1)}) %all-gather.3.cloned.1.call-update) | async-done | bytes 12582928 | tf_op jit(solution)/shard_map/all_gather | solution.py:21
  153.2 19.9 %reshape.61 = bf16[48,128,1024]{2,1,0:T(8,128)(2,1)} reshape(bf16[512,12,1024]{2,1,0:T(8,128)(2,1)} %all-gather.3.cloned.1.call-done) | data formatting | bytes 25165824 | tf_op jit(solution)/shard_map/reshape | solution.py:22
  173.1 80.8 %while.10 = (s32[]{:T(128)}, bf16[6,1,1024,128]{2,3,0,1:T(8,128)(2,1)}, s32[6,16]{1,0:T(8,128)}, bf16[48,128,1024]{2,1,0:T(8,128)(2,1)}, s32[6,16]{1,0:T(8,128)}...) while((s32[]{:T(128)}, bf16[6,1,1024,128]{2,3,0,1:T(8,128)(2,1)}, s32[6,16]{1,0:T(8,128)}, ...), condition=%wide.region_1.2_spmd, body=%wide.region_0.1_spmd.sunk | while | flops 539100224 | bytes 14423509 | solution.py:30
  173.8 7.3 %gather_fusion = bf16[16,128,1024]{2,1,0:T(8,128)(2,1)} fusion(bf16[48,128,1024]{2,1,0:T(8,128)(2,1)} %get-tuple-element.104, s32[1024]{0:T(1024)S(1)} %pad_clamp_fusion.2), kind=kCustom, calls=%fused_computation.clone.1 | custom fusion | bytes 8388672 | tf_op jit(solution)/shard_map/while/body/eval_jaxpr/gather | solution.py:26
  181.9 3.9 fusion.32
  187.3 7.3 %gather_fusion = bf16[16,128,1024]{2,1,0:T(8,128)(2,1)} fusion(bf16[48,128,1024]{2,1,0:T(8,128)(2,1)} %get-tuple-element.104, s32[1024]{0:T(1024)S(1)} %pad_clamp_fusion.2), kind=kCustom, calls=%fused_computation.clone.1 | custom fusion | bytes 8388672 | tf_op jit(solution)/shard_map/while/body/eval_jaxpr/gather | solution.py:26
  195.3 3.9 fusion.32
  199.3 0.7 constant_dynamic-update-slice_fusion.2
  200.8 7.3 %gather_fusion = bf16[16,128,1024]{2,1,0:T(8,128)(2,1)} fusion(bf16[48,128,1024]{2,1,0:T(8,128)(2,1)} %get-tuple-element.104, s32[1024]{0:T(1024)S(1)} %pad_clamp_fusion.2), kind=kCustom, calls=%fused_computation.clone.1 | custom fusion | bytes 8388672 | tf_op jit(solution)/shard_map/while/body/eval_jaxpr/gather | solution.py:26
  208.8 3.9 fusion.32
  212.8 0.7 constant_dynamic-update-slice_fusion.2
  214.3 7.3 %gather_fusion = bf16[16,128,1024]{2,1,0:T(8,128)(2,1)} fusion(bf16[48,128,1024]{2,1,0:T(8,128)(2,1)} %get-tuple-element.104, s32[1024]{0:T(1024)S(1)} %pad_clamp_fusion.2), kind=kCustom, calls=%fused_computation.clone.1 | custom fusion | bytes 8388672 | tf_op jit(solution)/shard_map/while/body/eval_jaxpr/gather | solution.py:26
  222.3 3.9 fusion.32
  227.7 7.3 %gather_fusion = bf16[16,128,1024]{2,1,0:T(8,128)(2,1)} fusion(bf16[48,128,1024]{2,1,0:T(8,128)(2,1)} %get-tuple-element.104, s32[1024]{0:T(1024)S(1)} %pad_clamp_fusion.2), kind=kCustom, calls=%fused_computation.clone.1 | custom fusion | bytes 8388672 | tf_op jit(solution)/shard_map/while/body/eval_jaxpr/gather | solution.py:26
  235.7 3.9 fusion.32
  241.2 7.3 %gather_fusion = bf16[16,128,1024]{2,1,0:T(8,128)(2,1)} fusion(bf16[48,128,1024]{2,1,0:T(8,128)(2,1)} %get-tuple-element.104, s32[1024]{0:T(1024)S(1)} %pad_clamp_fusion.2), kind=kCustom, calls=%fused_computation.clone.1 | custom fusion | bytes 8388672 | tf_op jit(solution)/shard_map/while/body/eval_jaxpr/gather | solution.py:26
  249.2 3.9 fusion.32
  253.9 7.4 %copy.14 = bf16[1,1024,768]{2,0,1:T(2,128)(2,1)S(1)} copy(bf16[1,1024,768]{1,2,0:T(8,128)(2,1)} %bitcast.55) | data formatting | bytes 3145728 | tf_op jit(solution)/shard_map/reshape | solution.py:31
  261.8 11.4 %reduce.2 = bf16[1024,768]{1,0:T(8,128)(2,1)} reduce(bf16[1024,1,768]{2,1,0:T(2,128)(2,1)S(1)} %bitcast.52, bf16[]{:T(256)} %broadcast.27), dimensions={1}, to_apply=%bitcast.31.reduce_sub_computation | reduce | bytes 3145730
  273.2 4.6 reshape.80
  277.8 8.9 %all-to-all-start = ((bf16[64,2,6144]{2,1,0:T(2,128)(2,1)}), bf16[64,2,6144]{2,1,0:T(2,128)(2,1)}, u32[]{:S(2)}, u32[]{:S(2)}) async-start(bf16[64,2,6144]{2,1,0:T(2,128)(2,1)} %reshape.80), calls=%async_computation | async-start | bytes 3145728 | tf_op jit(solution)/shard_map/all_to_all | solution.py:32
  287.0 38.9 %all-to-all-done = bf16[64,2,6144]{2,1,0:T(2,128)(2,1)} async-done(((bf16[64,2,6144]{2,1,0:T(2,128)(2,1)}), bf16[64,2,6144]{2,1,0:T(2,128)(2,1)}, u32[]{:S(2)}, u32[]{:S(2)}) %all-to-all-start) | async-done | bytes 1572896 | tf_op jit(solution)/shard_map/all_to_all | solution.py:32
  325.9 9.1 %reshape.81 = bf16[1024,1,768]{2,1,0:T(2,128)(2,1)S(1)} reshape(bf16[64,2,6144]{2,1,0:T(2,128)(2,1)} %all-to-all-done) | data formatting | bytes 3145728
  335.0 10.5 %bitcast_reduce_fusion = bf16[1024,768]{1,0:T(8,128)(2,1)} fusion(bf16[1024,1,768]{2,1,0:T(2,128)(2,1)S(1)} %reshape.81), kind=kLoop, calls=%fused_computation.23 | loop fusion | bytes 3145728 | tf_op jit(solution)/shard_map/all_to_all | solution.py:32
  345.5 2.8 reshape.63
  349.2 1.1 slice_select_fusion
  350.3 0.8 reshape_reshape.3
  351.1 67.3 %all-reduce.4.cloned.1.call-done = bf16[1024,512]{1,0:T(8,128)(2,1)} async-done(((bf16[1024,512]{1,0:T(8,128)(2,1)}), bf16[1024,512]{1,0:T(8,128)(2,1)}) %all-reduce.4.cloned.1.call-update) | async-done | bytes 1048592 | tf_op jit(solution)/shard_map/psum | solution.py:13
  418.3 3.4 convolution_multiply_fusion
  421.8 1.3 dynamic-slice
  423.7 157.0 %all-reduce.6.cloned.1.call-done = f32[512,768]{1,0:T(8,128)} async-done(((f32[512,768]{1,0:T(8,128)}), f32[512,768]{1,0:T(8,128)}) %all-reduce.6.cloned.1.call-update) | async-done | bytes 1572880
  580.7 1.3 constant_dynamic-slice_fusion.2
  (40 shorter events, 14.6 us)
Async XLA Ops:
  6.5 341.8 %copy-start = (bf16[64,64]{1,0:T(8,128)(2,1)S(1)}, bf16[64,64]{1,0:T(8,128)(2,1)}, u32[]{:S(2)}) copy-start(bf16[64,64]{1,0:T(8,128)(2,1)} %param.9) | copy-start | bytes 24580
  6.5 146.7 %all-gather.3.cloned.1.call-start = ((), (), s32[]{:S(2)}) async-start(), calls=%async_computation.2 | async-start | bytes 16809984 | tf_op jit(solution)/shard_map/all_gather | solution.py:21
  277.8 48.1 %all-to-all-start = ((bf16[64,2,6144]{2,1,0:T(2,128)(2,1)}), bf16[64,2,6144]{2,1,0:T(2,128)(2,1)}, u32[]{:S(2)}, u32[]{:S(2)}) async-start(bf16[64,2,6144]{2,1,0:T(2,128)(2,1)} %reshape.80), calls=%async_computation | async-start | bytes 3145728 | tf_op jit(solution)/shard_map/all_to_all | solution.py:32
  286.7 131.6 %all-reduce.4.cloned.1.call-start = ((), (), s32[]{:S(2)}) async-start(), calls=%async_computation.1 | async-start | bytes 2097152 | tf_op jit(solution)/shard_map/psum | solution.py:13
  350.3 230.5 %all-reduce.6.cloned.1.call-start = ((), (), s32[]{:S(2)}) async-start(), calls=%async_computation.3 | async-start | bytes 3145728
Sparse Core Ops, SparseCore 0:
  12.0 141.2 all-gather.2
  350.4 67.9 all-reduce.3
  421.9 158.7 all-reduce.5
where the time goes:
time: 593 us; the launch traced here: 589 us
  waiting for transfers between devices  410 us (69%)
  local copies, waits for them, and re-layouts  108 us (18%)
  matrix products  27.1 us (5%)
  other arithmetic  20.8 us (4%)
  between operations  13.8 us (2%)
  starting transfers between devices  9.21 us (2%)
    unnamed x4, waiting for transfers between devices  158 us
    all_gather x1, waiting for transfers between devices, on_device(): gathered = lax.all_gather(coefficients, ('aux', 'bas'), axis=0, tiled=True)  146 us
    psum x1, waiting for transfers between devices, spread(): return lax.psum(jnp.where(mine, value, jnp.zeros_like(value)), axis)  67.3 us
    gather x6, local copies, waits for them, and re-layouts, one_row(): picked = coeff_tiles[lam_row] * live_row.astype(jnp.bfloat16)[:, None, None]  43.9 us
    all_to_all x1, waiting for transfers between devices, on_device(): lax.all_to_all(half_done, 'aux', split_axis=1, concat_axis=0, tiled=True)  38.9 us
    dot_general x6, matrix products, one_row(): jnp.einsum('pzab,zbo->poa', ints_row, picked, preferred_element_type=jnp....  23.1 us
    reshape x1, local copies, waits for them, and re-layouts, on_device(): gathered.reshape(gathered.shape[0] // tile_size, tile_size, orbitals)  19.9 us
    unnamed x8, local copies, waits for them, and re-layouts  17.2 us
  transfers between devices with their start and end apart: 4, of which 4 were waited for; matrix products, arithmetic and copies ran while one was open for 0% of the time, Pallas kernels for 0%

commit v1 on v0

v1 whole, which is shorter than its diff:
```python
import functools
import math

import jax
import jax.numpy as jnp
from jax import lax
from jax.experimental import pallas as pl
from jax.experimental.pallas import tpu as pltpu
from jax.sharding import PartitionSpec as P

BF16 = jnp.bfloat16
F32 = jnp.float32
GROUPS = 4
GRAN = 32


def kernel(
    dims,
    ints_hbm,
    coef_ref,
    metric_ref,
    tab_smem,
    tab_vmem,
    out_ref,
    ints,
    raw_f32,
    raw_send,
    raw_recv,
    join_f32,
    coeff,
    kron,
    win,
    win_tiles,
    mid_a,
    mixin,
    mixed,
    mid_b,
    imix_tiles,
    imix,
    tab_land,
    tab_win,
    wfull,
    half,
    exch,
    send_a,
    recv_a,
    send_b,
    recv_b,
    send_a2,
    recv_a2,
    send_b2,
    recv_b2,
    local_sem,
    raw_ssem,
    raw_rsem,
    scat_ssem,
    scat_rsem,
    ph2_ssem,
    ph2_rsem,
    ring_ssem,
    ring_rsem,
    sib_ssem,
    sib_rsem,
    a2a_ssem,
    a2a_rsem,
    w_ssem,
    w_rsem,
    ws_ssem,
    ws_rsem,
    rs_ssem,
    rs_rsem,
):
    zn, yn, xn, bs, nz, nrow, occ, krows, rows_dev, nb = dims
    bas_n = 2 * xn
    aux_n = zn * yn
    block = rows_dev * bas_n
    gcol = occ // GROUPS
    ms = krows // bas_n
    out_rows = krows // aux_n
    ncol = nrow * bs
    hcol = ncol // 2
    dead = nb // bs

    aux = lax.axis_index("aux")
    bas = lax.axis_index("bas")
    z, y = aux // yn, lax.rem(aux, yn)
    x, c = bas // 2, lax.rem(bas, 2)
    sib = (aux, x * 2 + 1 - c)

    def at_y(k):
        return (z * yn + lax.rem(y + k, yn), bas)

    def at_z(k):
        return (lax.rem(z + k, zn) * yn + y, bas)

    def at_bas(k):
        return (aux, lax.rem(bas + k, bas_n))

    def at_x(k):
        return (aux, lax.rem(x + k, xn) * 2 + c)

    def remote(src, dst, ssem, rsem, dev):
        return pltpu.make_async_remote_copy(
            src_ref=src, dst_ref=dst, send_sem=ssem, recv_sem=rsem,
            device_id=dev, device_id_type=pl.DeviceIdType.MESH)

    barrier = pltpu.get_barrier_semaphore()
    for k in range(1, yn):
        pl.semaphore_signal(barrier, inc=1, device_id=at_y(k), device_id_type=pl.DeviceIdType.MESH)
    for k in range(1, zn):
        pl.semaphore_signal(barrier, inc=1, device_id=at_z(k), device_id_type=pl.DeviceIdType.MESH)
    for k in range(1, bas_n):
        pl.semaphore_signal(barrier, inc=1, device_id=at_bas(k), device_id_type=pl.DeviceIdType.MESH)

    fetch = pltpu.make_async_copy(ints_hbm, ints, local_sem.at[0])
    fetch.start()
    raw_f32[...] = jnp.zeros_like(raw_f32)
    raw_f32[0:rows_dev, :] = coef_ref[...].astype(F32)
    packed = raw_f32[...].astype(BF16)
    raw_send[0] = packed[:, : occ // 2]
    raw_send[1] = packed[:, occ // 2 :]
    pl.semaphore_wait(barrier, yn - 1 + zn - 1 + bas_n - 1)

    def raw_copy(k):
        to = lax.rem(bas + k, bas_n)
        return remote(raw_send.at[lax.rem(to, 2)], raw_recv.at[bas], raw_ssem.at[k], raw_rsem.at[k], (aux, to))

    for k in range(1, bas_n):
        raw_copy(k).start()
    raw_recv[bas] = raw_send[c]

    def win_src(j):
        b = (j * ms) // bs
        off = (j * ms) % bs
        return ints_hbm.at[b, :, pl.ds(off, ms), :]

    @pl.when(bas == 0)
    def _():
        for j in range(1, bas_n):
            remote(tab_vmem, tab_land, scat_ssem.at[j, 1], scat_rsem.at[1], (aux, j)).start()
            remote(win_src(j), win, scat_ssem.at[j, 0], scat_rsem.at[0], (aux, j)).start()
        pltpu.make_async_copy(tab_vmem, tab_land, local_sem.at[2]).start()
        pltpu.make_async_copy(win_src(0), win, local_sem.at[1]).start()

    metric = metric_ref[...]
    gram = lax.dot_general(metric, metric, (((0,), (0,)), ((), ())), preferred_element_type=F32).astype(BF16)
    krow = yn * 16
    spread_c = (
        lax.broadcasted_iota(jnp.int32, (aux_n, aux_n * 16), 0)
        == (lax.broadcasted_iota(jnp.int32, (aux_n, aux_n * 16), 1) >> 4)
    ).astype(F32).astype(BF16)

    def kron_step(t, carry):
        r0 = pl.multiple_of(t * krow, krow)
        spread_r = (
            ((lax.broadcasted_iota(jnp.int32, (krow, aux_n), 0) + r0) >> 4)
            == lax.broadcasted_iota(jnp.int32, (krow, aux_n), 1)
        ).astype(F32).astype(BF16)
        rows = jnp.dot(spread_r, gram, preferred_element_type=F32).astype(BF16)
        full = jnp.dot(rows, spread_c, preferred_element_type=F32)
        same = (lax.broadcasted_iota(jnp.int32, full.shape, 0) & 15) == (
            lax.broadcasted_iota(jnp.int32, full.shape, 1) & 15)
        kron[pl.ds(r0, krow), :] = jnp.where(same, full, 0.0).astype(BF16)
        return carry

    lax.fori_loop(0, aux_n * 16 // krow, kron_step, 0)
    for g in range(GROUPS):
        coeff[g, nb // GRAN : (nb + bs) // GRAN] = jnp.zeros((bs // GRAN, GRAN, gcol), BF16)

    for k in range(1, bas_n):
        raw_copy(k).wait()
    for j in range(bas_n):
        join_f32[j * rows_dev : (j + 1) * rows_dev, :] = raw_recv[j][0:rows_dev, :].astype(F32)
    joined = join_f32[...].astype(BF16)
    per = block // GRAN
    coeff[2 * c, pl.ds(aux * per, per)] = joined[:, :gcol].reshape(per, GRAN, gcol)
    coeff[2 * c + 1, pl.ds(aux * per, per)] = joined[:, gcol:].reshape(per, GRAN, gcol)

    def at_block(st, zz, yy):
        return coeff.at[2 * c + st, pl.ds((zz * yn + yy) * per, per)]

    def ph2_copy(st, k):
        ref = at_block(st, z, y)
        return remote(ref, ref, ph2_ssem.at[st, k], ph2_rsem.at[st, k], at_z(k) if st == 0 else at_y(k))

    for k in range(1, max(zn, yn)):
        if k < zn:
            ph2_copy(0, k).start()
        if k < yn:
            ph2_copy(1, k).start()

    def slab_block(st, pos, q):
        return at_block(st, q, pos) if st == 0 else at_block(st, pos, q)

    def ring_copy(st, q, s):
        n, me, at = (yn, y, at_y) if st == 0 else (zn, z, at_z)
        m = zn if st == 0 else yn
        if isinstance(q, int):
            right = 1 if q < m // 2 else n - 1
        else:
            right = jnp.where(q < m // 2, 1, n - 1)
        pos = lax.rem(me + s * (n - right), n)
        ref = slab_block(st, pos, q)
        return remote(ref, ref, ring_ssem.at[st, q, s], ring_rsem.at[st, q, s], at(right))

    def sib_copy(st, q, s):
        n, me = (yn, y) if st == 0 else (zn, z)
        m = zn if st == 0 else yn
        if isinstance(q, int):
            right = 1 if q < m // 2 else n - 1
        else:
            right = jnp.where(q < m // 2, 1, n - 1)
        ref = slab_block(st, lax.rem(me + s * (n - right), n), q)
        return remote(ref, ref, sib_ssem.at[st, q, s], sib_rsem.at[st, q, s], sib)

    every = [(st, q) for i in range(max(zn, yn) // 2) for st in range(2)
             for q in (i, i + (zn if st == 0 else yn) // 2)]
    steps = yn - 1

    def ring_step(s, carry):
        for st, q in every:
            ring_copy(st, q, s).wait_recv()
            ring_copy(st, q, s + 1).start()
            sib_copy(st, q, s + 1).start()
        return carry

    def a2a_y(i, src, mid, k):
        to = lax.rem(y + k, yn)
        return remote(src.at[:, to], mid.at[y], a2a_ssem.at[i, 0, k], a2a_rsem.at[i, 0, k], at_y(k))

    def a2a_z(i, mid, dst, k):
        to = lax.rem(z + k, zn)
        return remote(mid.at[:, to], dst.at[z], a2a_ssem.at[i, 1, k], a2a_rsem.at[i, 1, k], at_z(k))

    def a2a_y_start(i, src, mid):
        for k in range(1, yn):
            a2a_y(i, src, mid, k).start()
        mid[y] = src[:, y]

    def a2a_z_start(i, src, mid, dst):
        for k in range(1, yn):
            a2a_y(i, src, mid, k).wait()
        for k in range(1, zn):
            a2a_z(i, mid, dst, k).start()
        dst[z] = mid[:, z]

    def a2a_end(i, mid, dst):
        for k in range(1, zn):
            a2a_z(i, mid, dst, k).wait()

    @pl.when(bas == 0)
    def _():
        pltpu.make_async_copy(tab_vmem, tab_land, local_sem.at[2]).wait()
        pltpu.make_async_copy(win_src(0), win, local_sem.at[1]).wait()

    @pl.when(bas != 0)
    def _():
        remote(tab_vmem, tab_land, scat_ssem.at[0, 1], scat_rsem.at[1], (aux, 0)).wait_recv()
        remote(win_src(0), win, scat_ssem.at[0, 0], scat_rsem.at[0], (aux, 0)).wait_recv()

    win_tiles[...] = win[...].reshape(zn, yn, 16, bs)
    a2a_y_start(0, win_tiles, mid_a)
    to_smem = pltpu.make_async_copy(tab_land, tab_win, local_sem.at[3])
    to_smem.start()

    for st, q0 in ((0, z), (1, y)):
        ring_copy(st, q0, 0).start()
        sib_copy(st, q0, 0).start()
    for k in range(1, max(zn, yn)):
        for st, q0, n in ((0, z, zn), (1, y, yn)):
            if k < n:
                ph2_copy(st, k).wait_recv()
                q = lax.rem(q0 + n - k, n)
                ring_copy(st, q, 0).start()
                sib_copy(st, q, 0).start()

    cut = [min(steps - 1, i) for i in (1, 2, 3, 4)]
    lax.fori_loop(0, cut[0], ring_step, 0)
    a2a_z_start(0, win_tiles, mid_a, mixin)
    lax.fori_loop(cut[0], cut[1], ring_step, 0)
    a2a_end(0, mid_a, mixin)

    def mix_step(t, carry):
        r0 = pl.multiple_of(t * krow, krow)
        rows = jnp.dot(
            kron[pl.ds(r0, krow), :], mixin[...].reshape(aux_n * 16, bs), preferred_element_type=F32)
        mixed[t] = rows.astype(BF16).reshape(yn, 16, bs)
        return carry

    lax.fori_loop(0, zn, mix_step, 0)
    a2a_y_start(1, mixed, mid_b)
    lax.fori_loop(cut[1], cut[2], ring_step, 0)
    a2a_z_start(1, mixed, mid_b, imix_tiles)
    lax.fori_loop(cut[2], steps - 1, ring_step, 0)
    a2a_end(1, mid_b, imix_tiles)
    imix[...] = imix_tiles[...].reshape(nz, ms, bs)
    for st, q in every:
        ring_copy(st, q, steps - 1).wait_recv()
        sib_copy(st, q, steps).start()
    fetch.wait()
    to_smem.wait()
    def sib_wait(s, carry):
        for st, q in every:
            sib_copy(st, q, s).wait_recv()
        return carry

    lax.fori_loop(0, steps + 1, sib_wait, 0)

    def block_of(g, index):
        return coeff[g, pl.ds(index * (bs // GRAN), bs // GRAN)].reshape(bs, gcol)

    wrow = (bas * ms) // bs

    def w_step(g, carry):
        acc = jnp.zeros((ms, gcol), F32)
        for s in range(0, nz, 2):
            lhs = jnp.concatenate([imix[s], imix[s + 1]], axis=1)
            rhs = jnp.concatenate([block_of(g, tab_win[wrow, s]), block_of(g, tab_win[wrow, s + 1])], axis=0)
            acc = acc + jnp.dot(lhs, rhs, preferred_element_type=F32)
        wfull[g, pl.ds(pl.multiple_of(bas * ms, 16), ms), :] = acc.astype(BF16)
        return carry

    lax.fori_loop(0, GROUPS, w_step, 0)

    def w_rows(j):
        return wfull.at[:, pl.ds(pl.multiple_of(j * ms, 16), ms), :]

    def w_copy(k):
        return remote(w_rows(bas), w_rows(bas), w_ssem.at[k], w_rsem.at[k], at_x(k))

    def ws_copy(k):
        j = lax.rem(x + k, xn) * 2 + c
        return remote(w_rows(j), w_rows(j), ws_ssem.at[k], ws_rsem.at[k], sib)

    for k in range(1, xn):
        w_copy(k).start()
    ws_copy(0).start()

    def half_step(t, carry):
        b, g = t // GROUPS, lax.rem(t, GROUPS)
        acc = jnp.zeros((bs, gcol), F32)
        for s in range(0, nz, 2):
            lhs = jnp.concatenate([ints[b, s], ints[b, s + 1]], axis=1)
            rhs = jnp.concatenate([block_of(g, tab_smem[b, s]), block_of(g, tab_smem[b, s + 1])], axis=0)
            acc = acc + jnp.dot(lhs, rhs, preferred_element_type=F32)
        half[g, pl.ds(pl.multiple_of(b * bs, bs), bs), :] = acc.astype(BF16)
        return carry

    half_total = nrow * GROUPS
    lax.fori_loop(0, half_total // 2, half_step, 0)
    for k in range(1, xn):
        w_copy(k).wait()
        ws_copy(xn - k).start()
    lax.fori_loop(half_total // 2, half_total, half_step, 0)
    for k in range(xn):
        ws_copy(k).wait()

    tn = 256 if ncol % 256 == 0 else 128

    def exch_step(t, carry):
        n0 = pl.multiple_of(t * tn, tn)
        acc = jnp.zeros((krows, tn), F32)
        for g in range(GROUPS):
            acc = acc + lax.dot_general(
                wfull[g], half[g, pl.ds(n0, tn), :], (((1,), (1,)), ((), ())), preferred_element_type=F32)
        exch[:, pl.ds(n0, tn)] = acc
        return carry

    lax.fori_loop(0, ncol // tn, exch_step, 0)

    chunk_a, chunk_b = zn * out_rows, yn * out_rows
    per_z = yn * out_rows

    for t in range(yn):
        rows = jnp.concatenate(
            [exch[zz * per_z + t * out_rows : zz * per_z + (t + 1) * out_rows, :hcol] for zz in range(zn)], axis=0)
        send_a[t] = rows.astype(BF16)
    for t in range(zn):
        send_b[t] = exch[t * per_z : (t + 1) * per_z, hcol:].astype(BF16)

    def rs_a(k):
        to = lax.rem(y + k, yn)
        return remote(send_a.at[to], recv_a.at[y], rs_ssem.at[0, k], rs_rsem.at[0, k], at_y(k))

    def rs_b(k):
        to = lax.rem(z + k, zn)
        return remote(send_b.at[to], recv_b.at[z], rs_ssem.at[1, k], rs_rsem.at[1, k], at_z(k))

    for k in range(1, max(yn, zn)):
        if k < yn:
            rs_a(k).start()
        if k < zn:
            rs_b(k).start()
    recv_a[y] = send_a[y]
    recv_b[z] = send_b[z]

    def total(ref, n):
        acc = ref[0].astype(F32)
        for i in range(1, n):
            acc = acc + ref[i].astype(F32)
        return acc

    for k in range(1, yn):
        rs_a(k).wait()
    sum_a = total(recv_a, yn)
    for t in range(zn):
        send_a2[t] = sum_a[t * out_rows : (t + 1) * out_rows, :]

    def rs_a2(k):
        to = lax.rem(z + k, zn)
        return remote(send_a2.at[to], recv_a2.at[z], rs_ssem.at[2, k], rs_rsem.at[2, k], at_z(k))

    for k in range(1, zn):
        rs_a2(k).start()
    recv_a2[z] = send_a2[z]

    for k in range(1, zn):
        rs_b(k).wait()
    sum_b = total(recv_b, zn)
    for t in range(yn):
        send_b2[t] = sum_b[t * out_rows : (t + 1) * out_rows, :]

    def rs_b2(k):
        to = lax.rem(y + k, yn)
        return remote(send_b2.at[to], recv_b2.at[y], rs_ssem.at[3, k], rs_rsem.at[3, k], at_y(k))

    for k in range(1, yn):
        rs_b2(k).start()
    recv_b2[y] = send_b2[y]

    @pl.when(bas == 0)
    def _():
        for j in range(1, bas_n):
            remote(tab_vmem, tab_land, scat_ssem.at[j, 1], scat_rsem.at[1], (aux, j)).wait_send()
            remote(win_src(j), win, scat_ssem.at[j, 0], scat_rsem.at[0], (aux, j)).wait_send()

    def drain(s, carry):
        for st, q in every:
            ring_copy(st, q, s).wait_send()
            sib_copy(st, q, s).wait_send()
        return carry

    lax.fori_loop(0, steps, drain, 0)
    for st, q in every:
        sib_copy(st, q, steps).wait_send()
    for k in range(1, max(zn, yn)):
        if k < zn:
            ph2_copy(0, k).wait_send()
        if k < yn:
            ph2_copy(1, k).wait_send()

    factor = 1.0 / math.sqrt(aux_n * occ)
    for k in range(1, zn):
        rs_a2(k).wait()
    out_ref[:, :hcol] = total(recv_a2, zn) * factor
    for k in range(1, yn):
        rs_b2(k).wait()
    out_ref[:, hcol:] = total(recv_b2, yn) * factor


def on_device(dims, integrals, coefficients, metric, pair_blocks, pair_live):
    zn, yn, xn, bs, nz, nrow, occ, krows, rows_dev, nb = dims
    bas_n, aux_n = 2 * xn, zn * yn
    block = rows_dev * bas_n
    gcol = occ // GROUPS
    ms = krows // bas_n
    out_rows = krows // aux_n
    ncol = nrow * bs
    hcol = ncol // 2
    pad = -(-rows_dev // 16) * 16
    table = jnp.where(pair_live > 0, pair_blocks, nb // bs).astype(jnp.int32)
    table = jnp.pad(table, ((0, 8 - nrow), (0, 128 - nz)))
    v, dma = pltpu.VMEM, pltpu.SemaphoreType.DMA
    most = max(yn, zn)
    steps = yn - 1
    return pl.pallas_call(
        functools.partial(kernel, dims),
        out_shape=jax.ShapeDtypeStruct((out_rows, ncol), F32),
        in_specs=[
            pl.BlockSpec(memory_space=pl.ANY),
            pl.BlockSpec(memory_space=pltpu.VMEM),
            pl.BlockSpec(memory_space=pltpu.VMEM),
            pl.BlockSpec(memory_space=pltpu.SMEM),
            pl.BlockSpec(memory_space=pltpu.VMEM),
        ],
        out_specs=pl.BlockSpec(memory_space=pltpu.VMEM),
        scratch_shapes=[
            v((nrow, nz, bs, bs), BF16),
            v((pad, occ), F32),
            v((2, pad, occ // 2), BF16),
            v((bas_n, pad, occ // 2), BF16),
            v((block, occ // 2), F32),
            v((GROUPS, (nb + bs) // GRAN, GRAN, gcol), BF16),
            v((aux_n * 16, aux_n * 16), BF16),
            v((nz, ms, bs), BF16),
            v((zn, yn, 16, bs), BF16),
            v((yn, zn, 16, bs), BF16),
            v((zn, yn, 16, bs), BF16),
            v((zn, yn, 16, bs), BF16),
            v((yn, zn, 16, bs), BF16),
            v((zn, yn, 16, bs), BF16),
            v((nz, ms, bs), BF16),
            v((8, 128), jnp.int32),
            pltpu.SMEM((8, 128), jnp.int32),
            v((GROUPS, krows, gcol), BF16),
            v((GROUPS, ncol, gcol), BF16),
            v((krows, ncol), F32),
            v((yn, zn * out_rows, hcol), BF16),
            v((yn, zn * out_rows, hcol), BF16),
            v((zn, yn * out_rows, hcol), BF16),
            v((zn, yn * out_rows, hcol), BF16),
            v((zn, out_rows, hcol), F32),
            v((zn, out_rows, hcol), F32),
            v((yn, out_rows, hcol), F32),
            v((yn, out_rows, hcol), F32),
            dma((4,)),
            dma((bas_n,)), dma((bas_n,)),
            dma((bas_n, 2)), dma((2,)),
            dma((2, most)), dma((2, most)),
            dma((2, most, steps)), dma((2, most, steps)),
            dma((2, most, steps + 1)), dma((2, most, steps + 1)),
            dma((2, 2, most)), dma((2, 2, most)),
            dma((xn,)), dma((xn,)),
            dma((xn,)), dma((xn,)),
            dma((4, most)), dma((4, most)),
        ],
        compiler_params=pltpu.CompilerParams(
            collective_id=0, has_side_effects=True, vmem_limit_bytes=52 * 1024 * 1024),
        cost_estimate=pl.CostEstimate(
            flops=2 * (nrow * nz * bs * bs * occ + krows * ncol * occ), bytes_accessed=4 * 1024 * 1024,
            transcendentals=0),
    )(integrals[0], coefficients, metric, table, table)


def solution(mesh, grid=(8, 8)):
    zn, yn = grid
    xn = mesh.shape["bas"] // 2

    def whole(integrals, coefficients, metric, pair_blocks, pair_live):
        bs, nz = integrals.shape[-1], integrals.shape[2]
        nb, occ = coefficients.shape
        nrow = integrals.shape[1] // (2 * xn)
        krows = 512 if nb == 6144 else 128
        dims = (zn, yn, xn, bs, nz, nrow, occ, krows, nb // mesh.size, nb)
        return jax.shard_map(
            functools.partial(on_device, dims),
            mesh=mesh,
            in_specs=(
                P("aux", "bas", None, None, None),
                P(("aux", "bas"), None),
                P(),
                P("bas", None),
                P("bas", None),
            ),
            out_specs=P("aux", "bas"),
            check_vma=False,
        )(integrals, coefficients, metric, pair_blocks, pair_live)

    return whole
```

time: 593 us -> 124 us (0.21)
  waiting for transfers between devices: 410 us -> 0 us
  Pallas kernels: 0 us -> 121 us
  local copies, waits for them, and re-layouts: 108 us -> 2.09 us
  matrix products: 27.1 us -> 0 us
  other arithmetic: 20.8 us -> 0.71 us
  between operations: 13.8 us -> 0.01 us
  starting transfers between devices: 9.21 us -> 0 us
    unnamed x4 -> x0, waiting for transfers between devices: 158 us -> none
    all_gather x1 -> x0, waiting for transfers between devices: 146 us -> none  [on_device(): gathered = lax.all_gather(coefficients, ('aux', 'bas'), axis=0, tiled=True)]
    pallas_call x0 -> x1, Pallas kernels: none -> 121 us  [on_device(): pl.pallas_call(functools.partial(kernel, dims), out_shape=jax.ShapeDtypeS...]
    psum x1 -> x0, waiting for transfers between devices: 67.3 us -> none  [spread(): return lax.psum(jnp.where(mine, value, jnp.zeros_like(value)), axis)]
    gather x6 -> x0, local copies, waits for them, and re-layouts: 43.9 us -> none  [one_row(): picked = coeff_tiles[lam_row] * live_row.astype(jnp.bfloat16)[:, None, None]]
    all_to_all x1 -> x0, waiting for transfers between devices: 38.9 us -> none  [on_device(): lax.all_to_all(half_done, 'aux', split_axis=1, concat_axis=0, tiled=True)]
    reshape x3 -> x0, local copies, waits for them, and re-layouts: 30.1 us -> none  [the longest x1 19.9 us: on_device(): gathered.reshape(gathered.shape[0] // tile_size, tile_size, orbitals)]
    dot_general x8 -> x0, matrix products: 27.1 us -> none  [the longest x6 23.1 us: one_row(): jnp.einsum('pzab,zbo->poa', ints_row, picked, preferred_element_type=jnp....]
  transfers between devices with their start and end apart: 4 -> 0, of which waited for: 4 -> 0; matrix products, arithmetic and copies ran while one was open for 0% -> 0% of each run, Pallas kernels for 0% -> 0%
where the time goes in v1:
time: 124 us
  Pallas kernels  121 us (98%)
  local copies, waits for them, and re-layouts  2.09 us (2%)
    pallas_call x1, Pallas kernels, on_device(): pl.pallas_call(functools.partial(kernel, dims), out_shape=jax.ShapeDtypeS...  121 us

profile of v1, /device:TPU:1, one launch (start us, length us, event | category | flops | bytes accessed | tf_op | source)
XLA Modules:
  0.0 124.2 jit_solution(10152733784810903892)
XLA Ops:
  0.0 0.7 compare_select_fusion
  0.7 0.0 copy-start
  0.7 0.8 copy-done
  1.5 0.0 copy-start.1
  1.5 0.7 copy-done.1
  2.2 121.4 %shard_map.55 = f32[8,768]{1,0:T(8,128)S(1)} custom-call(bf16[6,16,128,128]{3,2,1,0:T(8,128)(2,1)} %bitcast.1, bf16[12,1024]{1,0:T(8,128)(2,1)S(1)} %copy-done, bf16[64,64]{1,0:T(8,128)(2,1)S(1)} %copy-done.1, s32[8,128]{1,0:T(8,128)S(1)} %pad.4.tab_smem.tab_vmem, s32[8,128]{1,0:T(8,128)S(1)} %pad.4.tab_smem.tab_vmem), custom_call_target="tpu_custom_call" | custom-call | flops 4026531840 | bytes 4194304 | tf_op jit(solution)/shard_map/pallas_call | solution.py:476
  123.6 0.6 copy.7
  (1 shorter events, 0.0 us)
Async XLA Ops:
  0.7 0.8 copy-start
  1.5 0.7 copy-start.1

commit v2 on v1

v2 whole, which is shorter than its diff:
```python
import functools
import math

import jax
import jax.numpy as jnp
from jax import lax
from jax.experimental import pallas as pl
from jax.experimental.pallas import tpu as pltpu
from jax.sharding import PartitionSpec as P

BF16 = jnp.bfloat16
F32 = jnp.float32
GROUPS = 4
UNITS = 8
GRAN = 16
COMMON, PARITY = 1, 0


def wrap(value, n):
    assert n & (n - 1) == 0
    return value & (n - 1)


def kernel(
    dims,
    ints_hbm,
    coef_hbm,
    metric_hbm,
    blocks_hbm,
    live_hbm,
    out_ref,
    ints,
    coef_ref,
    metric_ref,
    raw_f32,
    raw_send,
    raw_recv,
    join_f32,
    coeff,
    kron,
    win,
    win_tiles,
    mid_a,
    mixin,
    mixed,
    mid_b,
    imix_tiles,
    imix,
    land_blocks,
    land_live,
    win_blocks,
    win_live,
    own_blocks,
    own_live,
    tab_z,
    tab_o,
    wfull,
    half,
    exch,
    send_a,
    recv_a,
    send_b,
    recv_b,
    send_a2,
    recv_a2,
    send_b2,
    recv_b2,
    local_sem,
    raw_ssem,
    raw_rsem,
    scat_ssem,
    scat_rsem,
    ph2_ssem,
    ph2_rsem,
    ring_ssem,
    ring_rsem,
    sib_ssem,
    sib_rsem,
    x_ssem,
    x_rsem,
    xsib_ssem,
    xsib_rsem,
    a2a_ssem,
    a2a_rsem,
    w_ssem,
    w_rsem,
    ws_ssem,
    ws_rsem,
    rs_ssem,
    rs_rsem,
):
    zn, yn, xn, bs, nz, nrow, occ, krows, rows_dev, nb = dims
    bas_n = 2 * xn
    aux_n = zn * yn
    block = rows_dev * bas_n
    gcol = occ // GROUPS
    ucol = occ // UNITS
    per = block // GRAN
    zh, yh = zn // 2, yn // 2
    ms = krows // bas_n
    out_rows = krows // aux_n
    ncol = nrow * bs
    hcol = ncol // 2
    dead = nb // bs

    aux = lax.axis_index("aux")
    bas = lax.axis_index("bas")
    y = wrap(aux, yn)
    z = (aux - y) // yn
    c = wrap(bas, 2)
    x = (bas - c) // 2
    par = wrap(x, 2)
    sib = (aux, x * 2 + 1 - c)

    def at_y(k):
        return (z * yn + wrap(y + k, yn), bas)

    def at_z(k):
        return (wrap(z + k, zn) * yn + y, bas)

    def at_bas(k):
        return (aux, wrap(bas + k, bas_n))

    def at_x(k):
        return (aux, wrap(x + k, xn) * 2 + c)

    def remote(src, dst, ssem, rsem, dev):
        return pltpu.make_async_remote_copy(
            src_ref=src, dst_ref=dst, send_sem=ssem, recv_sem=rsem,
            device_id=dev, device_id_type=pl.DeviceIdType.MESH)

    barrier = pltpu.get_barrier_semaphore()
    for k in range(1, yn):
        pl.semaphore_signal(barrier, inc=1, device_id=at_y(k), device_id_type=pl.DeviceIdType.MESH)
    for k in range(1, zn):
        pl.semaphore_signal(barrier, inc=1, device_id=at_z(k), device_id_type=pl.DeviceIdType.MESH)
    for k in range(1, bas_n):
        pl.semaphore_signal(barrier, inc=1, device_id=at_bas(k), device_id_type=pl.DeviceIdType.MESH)

    fetch_coef = pltpu.make_async_copy(coef_hbm, coef_ref, local_sem.at[6])
    fetch_coef.start()
    fetch_metric = pltpu.make_async_copy(metric_hbm, metric_ref, local_sem.at[7])
    fetch_metric.start()
    fetch = pltpu.make_async_copy(ints_hbm, ints, local_sem.at[0])
    fetch.start()
    own_tabs = [
        pltpu.make_async_copy(blocks_hbm, own_blocks, local_sem.at[3]),
        pltpu.make_async_copy(live_hbm, own_live, local_sem.at[4]),
    ]
    for copy in own_tabs:
        copy.start()
    raw_f32[...] = jnp.zeros_like(raw_f32)
    fetch_coef.wait()
    raw_f32[0:rows_dev, :] = coef_ref[...].astype(F32)
    packed = raw_f32[...].astype(BF16)
    raw_send[0] = packed[:, : occ // 2]
    raw_send[1] = packed[:, occ // 2 :]
    pl.semaphore_wait(barrier, yn - 1 + zn - 1 + bas_n - 1)

    def raw_copy(k):
        to = wrap(bas + k, bas_n)
        return remote(raw_send.at[wrap(to, 2)], raw_recv.at[bas], raw_ssem.at[k], raw_rsem.at[k], (aux, to))

    for k in range(1, bas_n):
        raw_copy(k).start()
    raw_recv[bas] = raw_send[c]

    def win_src(j):
        b = (j * ms) // bs
        off = (j * ms) % bs
        return ints_hbm.at[b, :, pl.ds(off, ms), :]

    def scatter(j):
        return [
            remote(blocks_hbm, land_blocks, scat_ssem.at[j, 1], scat_rsem.at[1], (aux, j)),
            remote(live_hbm, land_live, scat_ssem.at[j, 2], scat_rsem.at[2], (aux, j)),
            remote(win_src(j), win, scat_ssem.at[j, 0], scat_rsem.at[0], (aux, j)),
        ]

    @pl.when(bas == 0)
    def _():
        for j in range(1, bas_n):
            for copy in scatter(j):
                copy.start()
        pltpu.make_async_copy(blocks_hbm, land_blocks, local_sem.at[2]).start()
        pltpu.make_async_copy(live_hbm, land_live, local_sem.at[5]).start()
        pltpu.make_async_copy(win_src(0), win, local_sem.at[1]).start()

    for k in range(1, bas_n):
        raw_copy(k).wait()
    for j in range(bas_n):
        join_f32[j * rows_dev : (j + 1) * rows_dev, :] = raw_recv[j][0:rows_dev, :].astype(F32)

    def unit(st, kind):
        return 4 * c + st if kind == COMMON else 4 * c + 2 + par

    joined = join_f32[...].astype(BF16)
    cols = [joined[:, k * ucol : (k + 1) * ucol].reshape(per, GRAN, ucol) for k in range(4)]
    for st in range(2):
        coeff[unit(st, COMMON), z, pl.ds(y * per, per)] = cols[st]
    coeff[unit(0, PARITY), z, pl.ds(y * per, per)] = jnp.where(par == 0, cols[2], cols[3])

    def both(kind, run):
        if kind == COMMON:
            run(0)
            run(1)
        else:
            pl.when(c == 0)(lambda: run(0))
            pl.when(c == 1)(lambda: run(1))

    def ph2_copy(st, kind, k):
        ref = coeff.at[unit(st, kind), z, pl.ds(y * per, per)]
        return remote(
            ref, ref, ph2_ssem.at[st, kind, k], ph2_rsem.at[st, kind, k], at_z(k) if st == 0 else at_y(k))

    def near_first(n):
        return sorted(range(1, n), key=lambda k: min(k, n - k))

    def ph2_start(kind):
        def run(st):
            for k in near_first(zn if st == 0 else yn):
                ph2_copy(st, kind, k).start()
        both(kind, run)

    def ph2_drain(kind):
        def run(st):
            for k in range(1, zn if st == 0 else yn):
                ph2_copy(st, kind, k).wait_send()
        both(kind, run)

    ph2_start(PARITY)
    ph2_start(COMMON)

    def half_slab(u, st, d, h, s):
        n, me = (yn, y) if st == 0 else (zn, z)
        pos = wrap(me + (n - s if d == 0 else s), n)
        if st == 0:
            return coeff.at[u, pl.ds(h * zh, zh), pl.ds(pos * per, per)]
        return coeff.at[u, pos, pl.ds(h * yh * per, yh * per)]

    far = yn // 2

    def next_at(st, d):
        n, at = (yn, at_y) if st == 0 else (zn, at_z)
        return at(1) if d == 0 else at(n - 1)

    def ring_copy(st, kind, d, h, s):
        ref = half_slab(unit(st, kind), st, d, h, s)
        return remote(ref, ref, ring_ssem.at[st, kind, d], ring_rsem.at[st, kind, d, h, s], next_at(st, d))

    def ring_block(st, kind, q):
        zz, yy = (q, y) if st == 0 else (z, q)
        ref = coeff.at[unit(st, kind), zz, pl.ds(yy * per, per)]
        h = q // (zh if st == 0 else yh)
        for d in range(2):
            copy = remote(ref, ref, ring_ssem.at[st, kind, d], ring_rsem.at[st, kind, d, h, 0], next_at(st, d))
            if far > 1:
                copy.start()
            else:
                pl.when(h == d)(copy.start)

    def sib_copy(st, kind, d, h, s):
        ref = half_slab(unit(st, kind), st, d, h, s)
        return remote(ref, ref, sib_ssem.at[st, kind], sib_rsem.at[st, kind], sib)

    def x_copy(st, d, h, s):
        ref = half_slab(unit(st, PARITY), st, d, h, s)
        return remote(ref, ref, x_ssem.at[0], x_rsem.at[d, h, s], at_x(1) if h == 0 else at_x(xn - 1))

    def xsib_copy(st, d, h, s):
        ref = half_slab(4 * c + 3 - par, st, d, h, s)
        return remote(ref, ref, xsib_ssem.at[0], xsib_rsem.at[0], sib)

    def all_of(n, ssem, rsem):
        if n == 2 * zn:
            ref = coeff.at[0, pl.ds(0, zn)]
        else:
            ref = coeff.at[0, pl.ds(0, n), pl.ds(0, yh * per)]
        return remote(ref, ref, ssem, rsem, sib)

    def halves(s):
        if s == 0:
            return [(0, 0), (0, 1)]
        return [(d, h) for h in range(2) for d in range(2) if s < far or h == d]

    def own_slab():
        for kind in (PARITY, COMMON):
            both(kind, lambda st: ring_block(st, kind, z if st == 0 else y))
        for k in near_first(yn):
            for kind in (PARITY, COMMON):
                def run(st):
                    n, me = (zn, z) if st == 0 else (yn, y)
                    ph2_copy(st, kind, k).wait_recv()
                    ring_block(st, kind, wrap(me + n - k, n))
                both(kind, run)
        for kind in (PARITY, COMMON):
            arrive(kind, 0)

    def arrive(kind, s):
        def run(st):
            for d, h in halves(s):
                if s > 0:
                    ring_copy(st, kind, d, h, s - 1).wait_recv()
                    if s + 1 < far or (s + 1 == far and h == d):
                        ring_copy(st, kind, d, h, s).start()
                if kind == PARITY:
                    x_copy(st, d, h, s).start()
                sib_copy(st, kind, d, h, s).start()
        both(kind, run)

    def x_arrive(s):
        def run(st):
            for d, h in halves(s):
                x_copy(st, d, h, s).wait_recv()
                xsib_copy(st, d, h, s).start()
        both(PARITY, run)

    def sib_arrive(kind):
        def run(st):
            all_of(2 * zn, sib_ssem.at[st, kind], sib_rsem.at[st, kind]).wait_recv()
        if kind == COMMON:
            run(0)
            run(1)
        else:
            pl.when(c == 1)(lambda: run(0))
            pl.when(c == 0)(lambda: run(1))
            all_of(2 * zn, xsib_ssem.at[0], xsib_rsem.at[0]).wait_recv()

    def gather_drain(kind):
        def run(st):
            all_of(2 * zn, sib_ssem.at[st, kind], sib_rsem.at[st, kind]).wait_send()
            for d in range(2):
                all_of(yn - 1, ring_ssem.at[st, kind, d], ring_rsem.at[st, kind, d, 0, 0]).wait_send()
        if kind == PARITY:
            all_of(2 * zn, xsib_ssem.at[0], xsib_rsem.at[0]).wait_send()
            all_of(2 * zn, x_ssem.at[0], x_rsem.at[0, 0, 0]).wait_send()
        both(kind, run)
        ph2_drain(kind)

    krow = yn * 16

    def make_kron():
        fetch_metric.wait()
        metric = metric_ref[...]
        gram = lax.dot_general(metric, metric, (((0,), (0,)), ((), ())), preferred_element_type=F32).astype(BF16)
        spread_c = (
            lax.broadcasted_iota(jnp.int32, (aux_n, aux_n * 16), 0)
            == (lax.broadcasted_iota(jnp.int32, (aux_n, aux_n * 16), 1) >> 4)
        ).astype(F32).astype(BF16)

        def kron_step(t, carry):
            r0 = pl.multiple_of(t * krow, krow)
            spread_r = (
                ((lax.broadcasted_iota(jnp.int32, (krow, aux_n), 0) + r0) >> 4)
                == lax.broadcasted_iota(jnp.int32, (krow, aux_n), 1)
            ).astype(F32).astype(BF16)
            rows = jnp.dot(spread_r, gram, preferred_element_type=F32).astype(BF16)
            full = jnp.dot(rows, spread_c, preferred_element_type=F32)
            same = (lax.broadcasted_iota(jnp.int32, full.shape, 0) & 15) == (
                lax.broadcasted_iota(jnp.int32, full.shape, 1) & 15)
            kron[pl.ds(r0, krow), :] = jnp.where(same, full, 0.0).astype(BF16)
            return carry

        lax.fori_loop(0, aux_n * 16 // krow, kron_step, 0)
        for u in range(UNITS):
            coeff[u, zn, 0 : bs // GRAN] = jnp.zeros((bs // GRAN, GRAN, ucol), BF16)

    def a2a_y(i, src, mid, k):
        to = wrap(y + k, yn)
        return remote(src.at[:, to], mid.at[y], a2a_ssem.at[i, 0, k], a2a_rsem.at[i, 0, k], at_y(k))

    def a2a_z(i, mid, dst, k):
        to = wrap(z + k, zn)
        return remote(mid.at[:, to], dst.at[z], a2a_ssem.at[i, 1, k], a2a_rsem.at[i, 1, k], at_z(k))

    def a2a_y_start(i, src, mid):
        for k in range(1, yn):
            a2a_y(i, src, mid, k).start()
        mid[y] = src[:, y]

    def a2a_z_start(i, src, mid, dst):
        for k in range(1, yn):
            a2a_y(i, src, mid, k).wait()
        for k in range(1, zn):
            a2a_z(i, mid, dst, k).start()
        dst[z] = mid[:, z]

    def a2a_end(i, mid, dst):
        for k in range(1, zn):
            a2a_z(i, mid, dst, k).wait()

    def scatter_arrive():
        @pl.when(bas == 0)
        def _():
            pltpu.make_async_copy(blocks_hbm, land_blocks, local_sem.at[2]).wait()
            pltpu.make_async_copy(live_hbm, land_live, local_sem.at[5]).wait()
            pltpu.make_async_copy(win_src(0), win, local_sem.at[1]).wait()

        @pl.when(bas != 0)
        def _():
            for copy in scatter(0):
                copy.wait_recv()

        win_tiles[...] = win[...].reshape(zn, yn, 16, bs)

    per_z = yn * block // bs

    def tables():
        win_tabs = [
            pltpu.make_async_copy(land_blocks, win_blocks, local_sem.at[2]),
            pltpu.make_async_copy(land_live, win_live, local_sem.at[5]),
        ]
        for copy in win_tabs:
            copy.start()
        for copy in own_tabs + win_tabs:
            copy.wait()
        wrow = (bas * ms) // bs

        def fill(s, carry):
            for b in range(nrow + 1):
                if b < nrow:
                    blk, live = own_blocks[b, s], own_live[b, s]
                else:
                    blk, live = win_blocks[wrow, s], win_live[wrow, s]
                place = live * (blk - dead) + dead
                tab_z[b, s] = lax.div(place, per_z)
                tab_o[b, s] = lax.rem(place, per_z) * (bs // GRAN)
            return carry

        lax.fori_loop(0, nz, fill, 0)

    def mix():
        def mix_step(t, carry):
            r0 = pl.multiple_of(t * krow, krow)
            rows = jnp.dot(
                kron[pl.ds(r0, krow), :], mixin[...].reshape(aux_n * 16, bs), preferred_element_type=F32)
            mixed[t] = rows.astype(BF16).reshape(yn, 16, bs)
            return carry

        lax.fori_loop(0, zn, mix_step, 0)

    def chain(k):
        if k == CHAIN[0]:
            scatter_arrive()
            a2a_y_start(0, win_tiles, mid_a)
            make_kron()
        if k == CHAIN[1]:
            a2a_z_start(0, win_tiles, mid_a, mixin)
            tables()
        if k == CHAIN[2]:
            a2a_end(0, mid_a, mixin)
            mix()
            a2a_y_start(1, mixed, mid_b)
        if k == CHAIN[3]:
            a2a_z_start(1, mixed, mid_b, imix_tiles)

    CHAIN = [min(k, far) for k in (0, 1, 2, 3)]
    own_slab()
    chain(0)
    for k in range(1, far + 1):
        arrive(PARITY, k)
        arrive(COMMON, k)
        x_arrive(k - 1)
        chain(k)
    x_arrive(far)
    a2a_end(1, mid_b, imix_tiles)
    imix[...] = imix_tiles[...].reshape(nz, ms, bs)
    fetch.wait()
    sib_arrive(PARITY)
    sib_arrive(COMMON)

    def block_of(g, b, s):
        zi, off = tab_z[b, s], tab_o[b, s]
        return jnp.concatenate(
            [coeff[2 * g + i, zi, pl.ds(off, bs // GRAN)].reshape(bs, ucol) for i in range(2)], axis=1)

    def w_step(g, carry):
        acc = jnp.zeros((ms, gcol), F32)
        for s in range(0, nz, 2):
            lhs = jnp.concatenate([imix[s], imix[s + 1]], axis=1)
            rhs = jnp.concatenate([block_of(g, nrow, s), block_of(g, nrow, s + 1)], axis=0)
            acc = acc + jnp.dot(lhs, rhs, preferred_element_type=F32)
        wfull[g, pl.ds(pl.multiple_of(bas * ms, 16), ms), :] = acc.astype(BF16)
        return carry

    lax.fori_loop(0, GROUPS, w_step, 0)

    def w_rows(j):
        return wfull.at[:, pl.ds(pl.multiple_of(j * ms, 16), ms), :]

    def w_copy(k):
        return remote(w_rows(bas), w_rows(bas), w_ssem.at[k], w_rsem.at[k], at_x(k))

    def ws_copy(k):
        j = wrap(x + k, xn) * 2 + c
        return remote(w_rows(j), w_rows(j), ws_ssem.at[k], ws_rsem.at[k], sib)

    for k in range(1, xn):
        w_copy(k).start()
    ws_copy(0).start()

    def half_step(t, carry):
        b, g = t // GROUPS, lax.rem(t, GROUPS)
        acc = jnp.zeros((bs, gcol), F32)
        for s in range(0, nz, 2):
            lhs = jnp.concatenate([ints[b, s], ints[b, s + 1]], axis=1)
            rhs = jnp.concatenate([block_of(g, b, s), block_of(g, b, s + 1)], axis=0)
            acc = acc + jnp.dot(lhs, rhs, preferred_element_type=F32)
        half[g, pl.ds(pl.multiple_of(b * bs, bs), bs), :] = acc.astype(BF16)
        return carry

    half_total = nrow * GROUPS
    lax.fori_loop(0, half_total // 2, half_step, 0)
    for k in range(1, xn):
        w_copy(k).wait()
        ws_copy(xn - k).start()
    lax.fori_loop(half_total // 2, half_total, half_step, 0)
    for k in range(xn):
        ws_copy(k).wait()

    tn = 256 if ncol % 256 == 0 else 128

    def exch_step(t, carry):
        n0 = pl.multiple_of(t * tn, tn)
        acc = jnp.zeros((krows, tn), F32)
        for g in range(GROUPS):
            acc = acc + lax.dot_general(
                wfull[g], half[g, pl.ds(n0, tn), :], (((1,), (1,)), ((), ())), preferred_element_type=F32)
        exch[:, pl.ds(n0, tn)] = acc
        return carry

    lax.fori_loop(0, ncol // tn, exch_step, 0)

    zrows = yn * out_rows

    for t in range(yn):
        rows = jnp.concatenate(
            [exch[zz * zrows + t * out_rows : zz * zrows + (t + 1) * out_rows, :hcol] for zz in range(zn)], axis=0)
        send_a[t] = rows.astype(BF16)
    for t in range(zn):
        send_b[t] = exch[t * zrows : (t + 1) * zrows, hcol:].astype(BF16)

    def rs_a(k):
        to = wrap(y + k, yn)
        return remote(send_a.at[to], recv_a.at[y], rs_ssem.at[0, k], rs_rsem.at[0, k], at_y(k))

    def rs_b(k):
        to = wrap(z + k, zn)
        return remote(send_b.at[to], recv_b.at[z], rs_ssem.at[1, k], rs_rsem.at[1, k], at_z(k))

    for k in range(1, max(yn, zn)):
        if k < yn:
            rs_a(k).start()
        if k < zn:
            rs_b(k).start()
    recv_a[y] = send_a[y]
    recv_b[z] = send_b[z]

    @pl.when(bas == 0)
    def _():
        for j in range(1, bas_n):
            for copy in scatter(j):
                copy.wait_send()

    gather_drain(PARITY)
    gather_drain(COMMON)

    def total(ref, n):
        acc = ref[0].astype(F32)
        for i in range(1, n):
            acc = acc + ref[i].astype(F32)
        return acc

    for k in range(1, yn):
        rs_a(k).wait()
    sum_a = total(recv_a, yn)
    for t in range(zn):
        send_a2[t] = sum_a[t * out_rows : (t + 1) * out_rows, :]

    def rs_a2(k):
        to = wrap(z + k, zn)
        return remote(send_a2.at[to], recv_a2.at[z], rs_ssem.at[2, k], rs_rsem.at[2, k], at_z(k))

    for k in range(1, zn):
        rs_a2(k).start()
    recv_a2[z] = send_a2[z]

    for k in range(1, zn):
        rs_b(k).wait()
    sum_b = total(recv_b, zn)
    for t in range(yn):
        send_b2[t] = sum_b[t * out_rows : (t + 1) * out_rows, :]

    def rs_b2(k):
        to = wrap(y + k, yn)
        return remote(send_b2.at[to], recv_b2.at[y], rs_ssem.at[3, k], rs_rsem.at[3, k], at_y(k))

    for k in range(1, yn):
        rs_b2(k).start()
    recv_b2[y] = send_b2[y]

    factor = 1.0 / math.sqrt(aux_n * occ)
    for k in range(1, zn):
        rs_a2(k).wait()
    out_ref[:, :hcol] = total(recv_a2, zn) * factor
    for k in range(1, yn):
        rs_b2(k).wait()
    out_ref[:, hcol:] = total(recv_b2, yn) * factor


def on_device(dims, integrals, coefficients, metric, pair_blocks, pair_live):
    zn, yn, xn, bs, nz, nrow, occ, krows, rows_dev, nb = dims
    bas_n, aux_n = 2 * xn, zn * yn
    block = rows_dev * bas_n
    gcol = occ // GROUPS
    ms = krows // bas_n
    out_rows = krows // aux_n
    ncol = nrow * bs
    hcol = ncol // 2
    pad = -(-rows_dev // 16) * 16
    v, dma = pltpu.VMEM, pltpu.SemaphoreType.DMA
    most = max(yn, zn)
    return pl.pallas_call(
        functools.partial(kernel, dims),
        out_shape=jax.ShapeDtypeStruct((out_rows, ncol), F32),
        in_specs=[pl.BlockSpec(memory_space=pltpu.HBM)] * 5,
        out_specs=pl.BlockSpec(memory_space=pltpu.VMEM),
        scratch_shapes=[
            v((nrow, nz, bs, bs), BF16),
            v((rows_dev, occ), BF16),
            v((aux_n, aux_n), BF16),
            v((pad, occ), F32),
            v((2, pad, occ // 2), BF16),
            v((bas_n, pad, occ // 2), BF16),
            v((block, occ // 2), F32),
            v((UNITS, zn + 1, yn * block // GRAN, GRAN, occ // UNITS), BF16),
            v((aux_n * 16, aux_n * 16), BF16),
            v((nz, ms, bs), BF16),
            v((zn, yn, 16, bs), BF16),
            v((yn, zn, 16, bs), BF16),
            v((zn, yn, 16, bs), BF16),
            v((zn, yn, 16, bs), BF16),
            v((yn, zn, 16, bs), BF16),
            v((zn, yn, 16, bs), BF16),
            v((nz, ms, bs), BF16),
            v((nrow, nz), jnp.int32),
            v((nrow, nz), jnp.int32),
            pltpu.SMEM((nrow, nz), jnp.int32),
            pltpu.SMEM((nrow, nz), jnp.int32),
            pltpu.SMEM((nrow, nz), jnp.int32),
            pltpu.SMEM((nrow, nz), jnp.int32),
            pltpu.SMEM((nrow + 1, nz), jnp.int32),
            pltpu.SMEM((nrow + 1, nz), jnp.int32),
            v((GROUPS, krows, gcol), BF16),
            v((GROUPS, ncol, gcol), BF16),
            v((krows, ncol), F32),
            v((yn, zn * out_rows, hcol), BF16),
            v((yn, zn * out_rows, hcol), BF16),
            v((zn, yn * out_rows, hcol), BF16),
            v((zn, yn * out_rows, hcol), BF16),
            v((zn, out_rows, hcol), F32),
            v((zn, out_rows, hcol), F32),
            v((yn, out_rows, hcol), F32),
            v((yn, out_rows, hcol), F32),
            dma((8,)),
            dma((bas_n,)), dma((bas_n,)),
            dma((bas_n, 3)), dma((3,)),
            dma((2, 2, most)), dma((2, 2, most)),
            dma((2, 2, 2)), dma((2, 2, 2, 2, most)),
            dma((2, 2)), dma((2, 2)),
            dma((1,)), dma((2, 2, most)),
            dma((1,)), dma((1,)),
            dma((2, 2, most)), dma((2, 2, most)),
            dma((xn,)), dma((xn,)),
            dma((xn,)), dma((xn,)),
            dma((4, most)), dma((4, most)),
        ],
        compiler_params=pltpu.CompilerParams(
            collective_id=0, has_side_effects=True, vmem_limit_bytes=52 * 1024 * 1024),
        cost_estimate=pl.CostEstimate(
            flops=2 * (nrow * nz * bs * bs * occ + krows * ncol * occ), bytes_accessed=4 * 1024 * 1024,
            transcendentals=0),
    )(integrals[0], coefficients, metric, pair_blocks, pair_live)


def solution(mesh, grid=(8, 8)):
    zn, yn = grid
    xn = mesh.shape["bas"] // 2

    def whole(integrals, coefficients, metric, pair_blocks, pair_live):
        bs, nz = integrals.shape[-1], integrals.shape[2]
        nb, occ = coefficients.shape
        nrow = integrals.shape[1] // (2 * xn)
        krows = 512 if nb == 6144 else 128
        dims = (zn, yn, xn, bs, nz, nrow, occ, krows, nb // mesh.size, nb)
        return jax.shard_map(
            functools.partial(on_device, dims),
            mesh=mesh,
            in_specs=(
                P("aux", "bas", None, None, None),
                P(("aux", "bas"), None),
                P(),
                P("bas", None),
                P("bas", None),
            ),
            out_specs=P("aux", "bas"),
            check_vma=False,
        )(integrals, coefficients, metric, pair_blocks, pair_live)

    return whole
```

time: 124 us -> 104 us (0.84)
  Pallas kernels: 121 us -> 100 us
  local copies, waits for them, and re-layouts: 2.09 us -> 3.46 us
    pallas_call x1, Pallas kernels: 121 us -> 100 us  [on_device(): pl.pallas_call(functools.partial(kernel, dims), out_shape=jax.ShapeDtypeS...]
    unnamed x5 -> x9, local copies, waits for them, and re-layouts: 2.08 us -> 3.46 us
where the time goes in v2:
time: 104 us
  Pallas kernels  100 us (96%)
  local copies, waits for them, and re-layouts  3.46 us (3%)
    pallas_call x1, Pallas kernels, on_device(): pl.pallas_call(functools.partial(kernel, dims), out_shape=jax.ShapeDtypeS...  100 us
    unnamed x9, local copies, waits for them, and re-layouts  3.46 us

profile of v2, /device:TPU:1, one launch (start us, length us, event | category | flops | bytes accessed | tf_op | source)
XLA Modules:
  0.0 103.9 jit_solution(5087442655278608541)
XLA Ops:
  0.0 0.0 copy-start
  0.0 0.8 copy-done
  0.8 0.0 copy-start.1
  0.8 0.7 copy-done.1
  1.5 0.0 copy-start.2
  1.5 0.7 copy-done.2
  2.2 0.0 copy-start.3
  2.2 0.7 copy-done.3
  2.9 100.5 %shard_map.55 = f32[8,768]{1,0:T(8,128)S(1)} custom-call(bf16[6,16,128,128]{3,2,1,0:T(8,128)(2,1)} %bitcast.1, bf16[12,1024]{1,0:T(8,128)(2,1)S(1)} %copy-done, bf16[64,64]{1,0:T(8,128)(2,1)S(1)} %copy-done.1, s32[6,16]{1,0:T(8,128)S(1)} %copy-done.2, s32[6,16]{1,0:T(8,128)S(1)} %copy-done.3), custom_call_target="tpu_custom_call" | custom-call | flops 4026531840 | bytes 4194304 | tf_op jit(solution)/shard_map/pallas_call | solution.py:623
  103.3 0.6 copy.7
Async XLA Ops:
  0.0 0.8 copy-start
  0.8 0.7 copy-start.1
  1.5 0.7 copy-start.2
  2.2 0.7 copy-start.3

commit v3 on v2

--- a/solution.py
+++ b/solution.py
@@ -19,6 +19,10 @@
 def wrap(value, n):
     assert n & (n - 1) == 0
     return value & (n - 1)
+
+
+def far_first(n):
+    return sorted(range(1, n), key=lambda k: -min(k, n - k))
 
 
 def kernel(
@@ -88,6 +92,8 @@
     ws_rsem,
     rs_ssem,
     rs_rsem,
+    rsb_ssem,
+    rsb_rsem,
 ):
     zn, yn, xn, bs, nz, nrow, occ, krows, rows_dev, nb = dims
     bas_n = 2 * xn
@@ -99,6 +105,8 @@
     zh, yh = zn // 2, yn // 2
     ms = krows // bas_n
     out_rows = krows // aux_n
+    mh = ms // 2
+    assert ms == yn * out_rows
     ncol = nrow * bs
     hcol = ncol // 2
     dead = nb // bs
@@ -161,7 +169,7 @@
         to = wrap(bas + k, bas_n)
         return remote(raw_send.at[wrap(to, 2)], raw_recv.at[bas], raw_ssem.at[k], raw_rsem.at[k], (aux, to))
 
-    for k in range(1, bas_n):
+    for k in far_first(bas_n):
         raw_copy(k).start()
     raw_recv[bas] = raw_send[c]
 
@@ -228,8 +236,8 @@
                 ph2_copy(st, kind, k).wait_send()
         both(kind, run)
 
+    ph2_start(COMMON)
     ph2_start(PARITY)
-    ph2_start(COMMON)
 
     def half_slab(u, st, d, h, s):
         n, me = (yn, y) if st == 0 else (zn, z)
@@ -284,16 +292,16 @@
         return [(d, h) for h in range(2) for d in range(2) if s < far or h == d]
 
     def own_slab():
-        for kind in (PARITY, COMMON):
+        for kind in (COMMON, PARITY):
             both(kind, lambda st: ring_block(st, kind, z if st == 0 else y))
         for k in near_first(yn):
-            for kind in (PARITY, COMMON):
+            for kind in (COMMON, PARITY):
                 def run(st):
                     n, me = (zn, z) if st == 0 else (yn, y)
                     ph2_copy(st, kind, k).wait_recv()
                     ring_block(st, kind, wrap(me + n - k, n))
                 both(kind, run)
-        for kind in (PARITY, COMMON):
+        for kind in (COMMON, PARITY):
             arrive(kind, 0)
 
     def arrive(kind, s):
@@ -374,14 +382,14 @@
         return remote(mid.at[:, to], dst.at[z], a2a_ssem.at[i, 1, k], a2a_rsem.at[i, 1, k], at_z(k))
 
     def a2a_y_start(i, src, mid):
-        for k in range(1, yn):
+        for k in far_first(yn):
             a2a_y(i, src, mid, k).start()
         mid[y] = src[:, y]
 
     def a2a_z_start(i, src, mid, dst):
         for k in range(1, yn):
             a2a_y(i, src, mid, k).wait()
-        for k in range(1, zn):
+        for k in far_first(zn):
             a2a_z(i, mid, dst, k).start()
         dst[z] = mid[:, z]
 
@@ -454,14 +462,15 @@
         if k == CHAIN[3]:
             a2a_z_start(1, mixed, mid_b, imix_tiles)
 
-    CHAIN = [min(k, far) for k in (0, 1, 2, 3)]
+    CHAIN = [min(k, 2 * far) for k in (0, 2, 4, 6)]
     own_slab()
     chain(0)
     for k in range(1, far + 1):
         arrive(PARITY, k)
+        chain(2 * k - 1)
         arrive(COMMON, k)
         x_arrive(k - 1)
-        chain(k)
+        chain(2 * k)
     x_arrive(far)
     a2a_end(1, mid_b, imix_tiles)
     imix[...] = imix_tiles[...].reshape(nz, ms, bs)
@@ -480,24 +489,29 @@
             lhs = jnp.concatenate([imix[s], imix[s + 1]], axis=1)
             rhs = jnp.concatenate([block_of(g, nrow, s), block_of(g, nrow, s + 1)], axis=0)
             acc = acc + jnp.dot(lhs, rhs, preferred_element_type=F32)
-        wfull[g, pl.ds(pl.multiple_of(bas * ms, 16), ms), :] = acc.astype(BF16)
+        for hf in range(2):
+            wfull[g, hf, bas] = acc[hf * mh : (hf + 1) * mh, :].astype(BF16)
         return carry
 
     lax.fori_loop(0, GROUPS, w_step, 0)
 
-    def w_rows(j):
-        return wfull.at[:, pl.ds(pl.multiple_of(j * ms, 16), ms), :]
-
-    def w_copy(k):
-        return remote(w_rows(bas), w_rows(bas), w_ssem.at[k], w_rsem.at[k], at_x(k))
-
-    def ws_copy(k):
-        j = wrap(x + k, xn) * 2 + c
-        return remote(w_rows(j), w_rows(j), ws_ssem.at[k], ws_rsem.at[k], sib)
-
-    for k in range(1, xn):
-        w_copy(k).start()
-    ws_copy(0).start()
+    def w_copy(hf, k):
+        ref = wfull.at[:, hf, bas]
+        return remote(ref, ref, w_ssem.at[hf, k], w_rsem.at[hf, k], at_x(k))
+
+    def ws_copy(hf, k):
+        ref = wfull.at[:, hf, wrap(x + k, xn) * 2 + c]
+        return remote(ref, ref, ws_ssem.at[hf, k], ws_rsem.at[hf, k], sib)
+
+    for hf in range(2):
+        for k in far_first(xn):
+            w_copy(hf, k).start()
+        ws_copy(hf, 0).start()
+
+    def w_pass_on(hf):
+        for k in range(1, xn):
+            w_copy(hf, k).wait()
+            ws_copy(hf, xn - k).start()
 
     def half_step(t, carry):
         b, g = t // GROUPS, lax.rem(t, GROUPS)
@@ -510,51 +524,51 @@
         return carry
 
     half_total = nrow * GROUPS
-    lax.fori_loop(0, half_total // 2, half_step, 0)
-    for k in range(1, xn):
-        w_copy(k).wait()
-        ws_copy(xn - k).start()
-    lax.fori_loop(half_total // 2, half_total, half_step, 0)
-    for k in range(xn):
-        ws_copy(k).wait()
+    lax.fori_loop(0, half_total * 4 // 5, half_step, 0)
+    w_pass_on(0)
+    lax.fori_loop(half_total * 4 // 5, half_total, half_step, 0)
 
     tn = 256 if ncol % 256 == 0 else 128
 
-    def exch_step(t, carry):
+    def exch_step(hf, t, carry):
         n0 = pl.multiple_of(t * tn, tn)
-        acc = jnp.zeros((krows, tn), F32)
+        acc = jnp.zeros((krows // 2, tn), F32)
         for g in range(GROUPS):
             acc = acc + lax.dot_general(
-                wfull[g], half[g, pl.ds(n0, tn), :], (((1,), (1,)), ((), ())), preferred_element_type=F32)
+                wfull[g, hf].reshape(krows // 2, gcol), half[g, pl.ds(n0, tn), :], (((1,), (1,)), ((), ())),
+                preferred_element_type=F32)
         exch[:, pl.ds(n0, tn)] = acc
         return carry
-
-    lax.fori_loop(0, ncol // tn, exch_step, 0)
-
-    zrows = yn * out_rows
-
-    for t in range(yn):
-        rows = jnp.concatenate(
-            [exch[zz * zrows + t * out_rows : zz * zrows + (t + 1) * out_rows, :hcol] for zz in range(zn)], axis=0)
-        send_a[t] = rows.astype(BF16)
-    for t in range(zn):
-        send_b[t] = exch[t * zrows : (t + 1) * zrows, hcol:].astype(BF16)
 
     def rs_a(k):
         to = wrap(y + k, yn)
         return remote(send_a.at[to], recv_a.at[y], rs_ssem.at[0, k], rs_rsem.at[0, k], at_y(k))
 
-    def rs_b(k):
+    def rs_b(hf, k):
         to = wrap(z + k, zn)
-        return remote(send_b.at[to], recv_b.at[z], rs_ssem.at[1, k], rs_rsem.at[1, k], at_z(k))
-
-    for k in range(1, max(yn, zn)):
-        if k < yn:
-            rs_a(k).start()
-        if k < zn:
-            rs_b(k).start()
+        return remote(send_b.at[hf, to], recv_b.at[hf, z], rsb_ssem.at[hf, k], rsb_rsem.at[hf, k], at_z(k))
+
+    def share(hf):
+        lax.fori_loop(0, ncol // tn, functools.partial(exch_step, hf), 0)
+        for t in range(zn):
+            send_b[hf, t] = exch[t * mh : (t + 1) * mh, hcol:].astype(BF16)
+        for k in far_first(zn):
+            rs_b(hf, k).start()
+        recv_b[hf, z] = send_b[hf, z]
+        for i in range(yh):
+            t = hf * yh + i
+            rows = jnp.concatenate(
+                [exch[zz * mh + i * out_rows : zz * mh + (i + 1) * out_rows, :hcol] for zz in range(zn)], axis=0)
+            send_a[t] = rows.astype(BF16)
+            pl.when(t != y)(lambda: rs_a(wrap(t - y + yn, yn)).start())
+
+    for hf in range(2):
+        if hf == 1:
+            w_pass_on(1)
+        for k in range(xn):
+            ws_copy(hf, k).wait()
+        share(hf)
     recv_a[y] = send_a[y]
-    recv_b[z] = send_b[z]
 
     @pl.when(bas == 0)
     def _():
@@ -581,21 +595,22 @@
         to = wrap(z + k, zn)
         return remote(send_a2.at[to], recv_a2.at[z], rs_ssem.at[2, k], rs_rsem.at[2, k], at_z(k))
 
-    for k in range(1, zn):
+    for k in far_first(zn):
         rs_a2(k).start()
     recv_a2[z] = send_a2[z]
 
-    for k in range(1, zn):
-        rs_b(k).wait()
-    sum_b = total(recv_b, zn)
-    for t in range(yn):
-        send_b2[t] = sum_b[t * out_rows : (t + 1) * out_rows, :]
+    for hf in range(2):
+        for k in range(1, zn):
+            rs_b(hf, k).wait()
+        sum_b = total(recv_b.at[hf], zn)
+        for i in range(yh):
+            send_b2[hf * yh + i] = sum_b[i * out_rows : (i + 1) * out_rows, :]
 
     def rs_b2(k):
         to = wrap(y + k, yn)
         return remote(send_b2.at[to], recv_b2.at[y], rs_ssem.at[3, k], rs_rsem.at[3, k], at_y(k))
 
-    for k in range(1, yn):
+    for k in far_first(yn):
         rs_b2(k).start()
     recv_b2[y] = send_b2[y]
 
@@ -615,6 +630,8 @@
     gcol = occ // GROUPS
     ms = krows // bas_n
     out_rows = krows // aux_n
+    mh = ms // 2
+    assert ms == yn * out_rows
     ncol = nrow * bs
     hcol = ncol // 2
     pad = -(-rows_dev // 16) * 16
@@ -651,13 +668,13 @@
             pltpu.SMEM((nrow, nz), jnp.int32),
             pltpu.SMEM((nrow + 1, nz), jnp.int32),
             pltpu.SMEM((nrow + 1, nz), jnp.int32),
-            v((GROUPS, krows, gcol), BF16),
+            v((GROUPS, 2, bas_n, ms // 2, gcol), BF16),
             v((GROUPS, ncol, gcol), BF16),
-            v((krows, ncol), F32),
+            v((krows // 2, ncol), F32),
             v((yn, zn * out_rows, hcol), BF16),
             v((yn, zn * out_rows, hcol), BF16),
-            v((zn, yn * out_rows, hcol), BF16),
-            v((zn, yn * out_rows, hcol), BF16),
+            v((2, zn, yn // 2 * out_rows, hcol), BF16),
+            v((2, zn, yn // 2 * out_rows, hcol), BF16),
             v((zn, out_rows, hcol), F32),
             v((zn, out_rows, hcol), F32),
             v((yn, out_rows, hcol), F32),
@@ -671,9 +688,10 @@
             dma((1,)), dma((2, 2, most)),
             dma((1,)), dma((1,)),
             dma((2, 2, most)), dma((2, 2, most)),
-            dma((xn,)), dma((xn,)),
-            dma((xn,)), dma((xn,)),
+            dma((2, xn)), dma((2, xn)),
+            dma((2, xn)), dma((2, xn)),
             dma((4, most)), dma((4, most)),
+            dma((2, most)), dma((2, most)),
         ],
         compiler_params=pltpu.CompilerParams(
             collective_id=0, has_side_effects=True, vmem_limit_bytes=52 * 1024 * 1024),

time: 104 us -> 101 us (0.971)
  Pallas kernels: 100 us -> 97.2 us
    pallas_call x1, Pallas kernels: 100 us -> 97.2 us  [on_device(): pl.pallas_call(functools.partial(kernel, dims), out_shape=jax.ShapeDtypeS...]
where the time goes in v3:
time: 101 us
  Pallas kernels  97.2 us (96%)
  local copies, waits for them, and re-layouts  3.46 us (3%)
    pallas_call x1, Pallas kernels, on_device(): pl.pallas_call(functools.partial(kernel, dims), out_shape=jax.ShapeDtypeS...  97.2 us
    unnamed x9, local copies, waits for them, and re-layouts  3.46 us

profile of v3, /device:TPU:1, one launch (start us, length us, event | category | flops | bytes accessed | tf_op | source)
XLA Modules:
  0.0 100.7 jit_solution(317505134925219212)
XLA Ops:
  0.0 0.0 copy-start
  0.0 0.8 copy-done
  0.8 0.0 copy-start.1
  0.8 0.7 copy-done.1
  1.5 0.0 copy-start.2
  1.5 0.7 copy-done.2
  2.2 0.0 copy-start.3
  2.2 0.7 copy-done.3
  2.9 97.2 %shard_map.55 = f32[8,768]{1,0:T(8,128)S(1)} custom-call(bf16[6,16,128,128]{3,2,1,0:T(8,128)(2,1)} %bitcast.1, bf16[12,1024]{1,0:T(8,128)(2,1)S(1)} %copy-done, bf16[64,64]{1,0:T(8,128)(2,1)S(1)} %copy-done.1, s32[6,16]{1,0:T(8,128)S(1)} %copy-done.2, s32[6,16]{1,0:T(8,128)S(1)} %copy-done.3), custom_call_target="tpu_custom_call" | custom-call | flops 4026531840 | bytes 4194304 | tf_op jit(solution)/shard_map/pallas_call | solution.py:640
  100.1 0.6 copy.7
Async XLA Ops:
  0.0 0.8 copy-start
  0.8 0.7 copy-start.1
  1.5 0.7 copy-start.2
  2.2 0.7 copy-start.3

commit v4 on v3

--- a/solution.py
+++ b/solution.py
@@ -226,9 +226,24 @@
 
     def ph2_start(kind):
         def run(st):
-            for k in near_first(zn if st == 0 else yn):
-                ph2_copy(st, kind, k).start()
+            n = zn if st == 0 else yn
+            for k in near_first(n):
+                if n != 8 or min(k, n - k) <= 2:
+                    ph2_copy(st, kind, k).start()
         both(kind, run)
+
+    def ph2_relay(st, kind, k):
+        n, me, at = (zn, z, at_z) if st == 0 else (yn, y, at_y)
+        if n != 8 or k not in (2, n - 2):
+            return
+        pos = wrap(me + n - k, n)
+        zz, yy = (pos, y) if st == 0 else (z, pos)
+        ref = coeff.at[unit(st, kind), zz, pl.ds(yy * per, per)]
+        up = (k == 2) == (st == kind)
+        for far_k in ((3, 4) if k == 2 else (n - 3, n - 4)):
+            if far_k == 4 and not up:
+                continue
+            remote(ref, ref, ph2_ssem.at[st, kind, far_k], ph2_rsem.at[st, kind, far_k], at(wrap(far_k - k + n, n))).start()
 
     def ph2_drain(kind):
         def run(st):
@@ -299,6 +314,7 @@
                 def run(st):
                     n, me = (zn, z) if st == 0 else (yn, y)
                     ph2_copy(st, kind, k).wait_recv()
+                    ph2_relay(st, kind, k)
                     ring_block(st, kind, wrap(me + n - k, n))
                 both(kind, run)
         for kind in (COMMON, PARITY):

time: 101 us -> 99.7 us (0.987)
  Pallas kernels: 97.2 us -> 95.9 us
    pallas_call x1, Pallas kernels: 97.2 us -> 95.9 us  [on_device(): pl.pallas_call(functools.partial(kernel, dims), out_shape=jax.ShapeDtypeS...]
where the time goes in v4:
time: 99.7 us; the launch traced here: 99.4 us
  Pallas kernels  95.9 us (96%)
  local copies, waits for them, and re-layouts  3.46 us (3%)
    pallas_call x1, Pallas kernels, on_device(): pl.pallas_call(functools.partial(kernel, dims), out_shape=jax.ShapeDtypeS...  95.9 us
    unnamed x9, local copies, waits for them, and re-layouts  3.46 us

profile of v4, /device:TPU:1, one launch (start us, length us, event | category | flops | bytes accessed | tf_op | source)
XLA Modules:
  0.0 99.4 jit_solution(14726286796728046845)
XLA Ops:
  0.0 0.0 copy-start
  0.0 0.8 copy-done
  0.8 0.0 copy-start.1
  0.8 0.7 copy-done.1
  1.5 0.0 copy-start.2
  1.5 0.7 copy-done.2
  2.2 0.0 copy-start.3
  2.2 0.7 copy-done.3
  2.9 95.9 %shard_map.55 = f32[8,768]{1,0:T(8,128)S(1)} custom-call(bf16[6,16,128,128]{3,2,1,0:T(8,128)(2,1)} %bitcast.1, bf16[12,1024]{1,0:T(8,128)(2,1)S(1)} %copy-done, bf16[64,64]{1,0:T(8,128)(2,1)S(1)} %copy-done.1, s32[6,16]{1,0:T(8,128)S(1)} %copy-done.2, s32[6,16]{1,0:T(8,128)S(1)} %copy-done.3), custom_call_target="tpu_custom_call" | custom-call | flops 4026531840 | bytes 4194304 | tf_op jit(solution)/shard_map/pallas_call | solution.py:656
  98.8 0.6 copy.7
Async XLA Ops:
  0.0 0.8 copy-start
  0.8 0.7 copy-start.1
  1.5 0.7 copy-start.2
  2.2 0.7 copy-start.3
